TPU v7x, 128 devices: a whole 4x4x4 slice. The times are simulated.
128 devices in a mesh: seq: 32 (over x, y_hi, z), dp: 4 (over y_lo, core).
Axes of the slice: x: 4, y: 4 (y_hi: 2, y_lo: 2; y = y_hi * 2 + y_lo), z: 4, core: 2. Of those that a mesh axis runs over, the one named last changes fastest.
Arguments:
- query: bfloat16 [4, 16384, 2048], P('dp', 'seq'), may hold values from -100 to 100
- key: bfloat16 [4, 16384, 2048], P('dp', 'seq'), may hold values from -6 to 6
- value: bfloat16 [4, 16384, 2048], P('dp', 'seq'), may hold values from -6 to 6
- grad_ctx: bfloat16 [4, 16384, 2048], P('dp', 'seq'), may hold values from -6 to 6
- proj_key: bfloat16 [512, 16384], P(None, 'seq'), may hold values from -0.046875 to 0.046875
- proj_value: bfloat16 [512, 16384], P(None, 'seq'), may hold values from -0.046875 to 0.046875
Outputs:
- grad_query: bfloat16 [4, 16384, 2048], P('dp', 'seq')
- grad_key: bfloat16 [4, 16384, 2048], P('dp', 'seq')
- grad_value: bfloat16 [4, 16384, 2048], P('dp', 'seq')
- grad_proj_key: bfloat16 [512, 16384], P('dp', 'seq')
- grad_proj_value: bfloat16 [512, 16384], P('dp', 'seq')
All inputs are finite; a program needn't handle non-finite values.
Results may differ from a plain program's by a relative error of at most 0.034.
The roundings to bfloat16 on the way count: a program that leaves them out, or rounds other values in their place, can miss the bound.
Values may be sent and summed in bfloat16 or wider, within the bound.
No kernel may reach another device: no remote copies, remote signals or barrier semaphores. Data moves between devices by JAX's collectives and lax.ppermute only.
A program may use at most 128 MiB of HBM per device.

v0:
```python
import jax
import jax.numpy as jnp
from jax import lax
from jax.sharding import PartitionSpec as P

H = 16
HEAD_DIM = 128


def head_pass(q, g, kp, vp):
    scale = HEAD_DIM ** (-0.5)
    hd_total = q.shape[1]
    rows = q.shape[0]
    gq = jnp.zeros((rows, hd_total), jnp.bfloat16)
    dkp = jnp.zeros((kp.shape[0], hd_total), jnp.float32)
    dvp = jnp.zeros((kp.shape[0], hd_total), jnp.float32)

    def per_head(h, carry):
        gq, dkp, dvp = carry
        start = h * HEAD_DIM
        q_head = lax.dynamic_slice_in_dim(q, start, HEAD_DIM, 1)
        g_head = lax.dynamic_slice_in_dim(g, start, HEAD_DIM, 1)
        kp_head = lax.dynamic_slice_in_dim(kp, start, HEAD_DIM, 1)
        vp_head = lax.dynamic_slice_in_dim(vp, start, HEAD_DIM, 1)
        scores = (
            lax.dot_general(
                q_head, kp_head, (((1,), (1,)), ((), ())), preferred_element_type=jnp.float32
            )
            * scale
        )
        probs = jax.nn.softmax(scores, axis=-1)
        probs_low = probs.astype(jnp.bfloat16)
        grad_probs = lax.dot_general(
            g_head, vp_head, (((1,), (1,)), ((), ())), preferred_element_type=jnp.float32
        )
        delta = jnp.sum(probs * grad_probs, axis=-1, keepdims=True)
        grad_scores = (probs * (grad_probs - delta) * scale).astype(jnp.bfloat16)
        gq_head = jnp.dot(grad_scores, kp_head, preferred_element_type=jnp.float32).astype(
            jnp.bfloat16
        )
        dkp_head = lax.dot_general(
            grad_scores, q_head, (((0,), (0,)), ((), ())), preferred_element_type=jnp.float32
        )
        dvp_head = lax.dot_general(
            probs_low, g_head, (((0,), (0,)), ((), ())), preferred_element_type=jnp.float32
        )
        gq = lax.dynamic_update_slice_in_dim(gq, gq_head, start, 1)
        dkp = lax.dynamic_update_slice_in_dim(dkp, dkp_head, start, 1)
        dvp = lax.dynamic_update_slice_in_dim(dvp, dvp_head, start, 1)
        return (gq, dkp, dvp)

    return lax.fori_loop(0, H, per_head, (gq, dkp, dvp))


def body(query, key, value, grad_ctx, proj_key, proj_value):
    q = query[0]
    k = key[0]
    v = value[0]
    g = grad_ctx[0]
    kp_part = jnp.dot(proj_key, k, preferred_element_type=jnp.float32)
    vp_part = jnp.dot(proj_value, v, preferred_element_type=jnp.float32)
    kp_full, vp_full = lax.psum((kp_part, vp_part), "seq")
    kp = kp_full.astype(jnp.bfloat16)
    vp = vp_full.astype(jnp.bfloat16)
    gq, dkp_part, dvp_part = head_pass(q, g, kp, vp)
    dkp_full, dvp_full = (
        lax.psum(dkp_part.astype(jnp.bfloat16), "seq").astype(jnp.float32),
        lax.psum(dvp_part.astype(jnp.bfloat16), "seq").astype(jnp.float32),
    )
    dkp = dkp_full.astype(jnp.bfloat16)
    dvp = dvp_full.astype(jnp.bfloat16)
    grad_k = lax.dot_general(
        proj_key, dkp, (((0,), (0,)), ((), ())), preferred_element_type=jnp.float32
    ).astype(jnp.bfloat16)
    grad_v = lax.dot_general(
        proj_value, dvp, (((0,), (0,)), ((), ())), preferred_element_type=jnp.float32
    ).astype(jnp.bfloat16)
    term_key = lax.dot_general(dkp, k, (((1,), (1,)), ((), ())), preferred_element_type=jnp.float32)
    term_value = lax.dot_general(
        dvp, v, (((1,), (1,)), ((), ())), preferred_element_type=jnp.float32
    )
    summed_key, summed_value = (
        lax.psum_scatter(
            term_key.astype(jnp.bfloat16), "dp", scatter_dimension=0, tiled=True
        ).astype(jnp.float32),
        lax.psum_scatter(
            term_value.astype(jnp.bfloat16), "dp", scatter_dimension=0, tiled=True
        ).astype(jnp.float32),
    )
    return (
        gq[None],
        grad_k[None],
        grad_v[None],
        summed_key.astype(jnp.bfloat16),
        summed_value.astype(jnp.bfloat16),
    )


def solution(mesh):
    return jax.shard_map(
        body,
        mesh=mesh,
        in_specs=(
            P("dp", "seq", None),
            P("dp", "seq", None),
            P("dp", "seq", None),
            P("dp", "seq", None),
            P(None, "seq"),
            P(None, "seq"),
        ),
        out_specs=(
            P("dp", "seq", None),
            P("dp", "seq", None),
            P("dp", "seq", None),
            P("dp", "seq"),
            P("dp", "seq"),
        ),
        check_vma=False,
    )
```

profile of v0, /device:TPU:1, one launch (start us, length us, event | category | flops | bytes accessed | tf_op | source)
XLA Modules:
  0.0 803.8 jit_solution(7639359778827727661)
XLA Ops:
  7.2 5.1 fusion.22
  12.4 3.2 fusion.26
  15.6 206.2 %all-reduce.6 = (bf16[512,2048]{1,0:T(8,128)(2,1)}, bf16[512,2048]{1,0:T(8,128)(2,1)}) all-reduce(f32[512,2048]{1,0:T(8,128)} %fusion.26, f32[512,2048]{1,0:T(8,128)} %fusion.22), channel_id=1, replica_groups=mesh['seq'=32,'dp'=4] {'seq'}, use_global_device_ids=true, to_apply=%region_0.0 | all-reduce | flops 2097152 | bytes 12582912 | tf_op jit(solution)/shard_map/psum | solution.py:62
  226.4 140.1 %while.17 = (s32[]{:T(128)}, bf16[512,2048]{1,0:T(8,128)(2,1)}, bf16[512,2048]{1,0:T(8,128)(2,1)}, bf16[512,2048]{1,0:T(8,128)(2,1)}, bf16[512,2048]{1,0:T(8,128...) while((s32[]{:T(128)}, bf16[512,2048]{1,0:T(8,128)(2,1)}, ...), condition=%wide.region_6.0_spmd, body=%wide.region_2.0_spmd.sunk | while | flops 340064768 | bytes 10513571 | solution.py:52
  227.9 1.9 convolution_dynamic-update-slice_fusion.5
  231.4 1.9 convolution_dynamic-update-slice_fusion.4
  233.3 1.9 fusion.62
  236.7 1.9 convolution_dynamic-update-slice_fusion.5
  240.2 1.9 convolution_dynamic-update-slice_fusion.4
  242.0 1.9 fusion.62
  245.4 1.9 convolution_dynamic-update-slice_fusion.5
  250.8 1.9 fusion.62
  254.2 1.9 convolution_dynamic-update-slice_fusion.5
  259.5 1.9 fusion.62
  262.9 1.9 convolution_dynamic-update-slice_fusion.5
  268.3 1.9 fusion.62
  271.7 1.9 convolution_dynamic-update-slice_fusion.5
  275.2 1.9 convolution_dynamic-update-slice_fusion.4
  277.0 1.9 fusion.62
  280.4 1.9 convolution_dynamic-update-slice_fusion.5
  285.8 1.9 fusion.62
  289.2 1.9 convolution_dynamic-update-slice_fusion.5
  294.6 1.9 fusion.62
  298.0 1.9 convolution_dynamic-update-slice_fusion.5
  303.3 1.9 fusion.62
  306.7 1.9 convolution_dynamic-update-slice_fusion.5
  312.1 1.9 fusion.62
  315.5 1.9 convolution_dynamic-update-slice_fusion.5
  320.8 1.9 fusion.62
  324.2 1.9 convolution_dynamic-update-slice_fusion.5
  329.6 1.9 fusion.62
  333.0 1.9 convolution_dynamic-update-slice_fusion.5
  338.3 1.9 fusion.62
  341.7 1.9 convolution_dynamic-update-slice_fusion.5
  347.1 1.9 fusion.62
  350.5 1.9 convolution_dynamic-update-slice_fusion.5
  355.8 1.9 fusion.62
  359.2 1.9 convolution_dynamic-update-slice_fusion.5
  364.6 1.9 fusion.62
  366.6 364.6 %all-reduce.5.cloned.1.call-done = (bf16[512,2048]{1,0:T(8,128)(2,1)}, bf16[512,2048]{1,0:T(8,128)(2,1)}) async-done(((bf16[512,2048]{1,0:T(8,128)(2,1)}, bf16[512,2048]{1,0:T(8,128)(2,1)}), (bf16[512,2048]{1,0:T(8,128)(2,1)}, bf16[512,2048]{1,0:T(8,128)(2,1)})) %all-reduce.5.cloned.1.call-update) | async-done | bytes 4194320 | tf_op jit(solution)/shard_map/psum | solution.py:67
  731.1 3.7 fusion.28
  734.9 4.3 fusion.31
  739.2 4.2 fusion.18
  743.4 4.0 copy.11
  747.4 4.2 fusion.19
  751.6 3.9 copy.12
  755.5 19.7 %reduce-scatter.3.cloned.1.call-done = bf16[128,512]{1,0:T(8,128)(2,1)} async-done(((bf16[512,512]{1,0:T(8,128)(2,1)}), bf16[128,512]{1,0:T(8,128)(2,1)}) %reduce-scatter.3.cloned.1.call-update) | async-done | bytes 131088 | tf_op jit(solution)/shard_map/reduce_scatter | solution.py:83
  775.2 22.1 %reduce-scatter.5.cloned.1.call-done = bf16[128,512]{1,0:T(8,128)(2,1)} async-done(((bf16[512,512]{1,0:T(8,128)(2,1)}), bf16[128,512]{1,0:T(8,128)(2,1)}) %reduce-scatter.5.cloned.1.call-update) | async-done | bytes 131088 | tf_op jit(solution)/shard_map/reduce_scatter | solution.py:86
  (92 shorter events, 78.1 us)
Async XLA Ops:
  7.2 5.2 copy-start
  7.2 5.2 copy-start.1
  7.2 723.9 %all-reduce.5.cloned.1.call-start = ((), (), s32[]{:S(2)}) async-start(), calls=%async_computation.4 | async-start | bytes 8388608 | tf_op jit(solution)/shard_map/psum | solution.py:67
  366.5 408.6 %reduce-scatter.3.cloned.1.call-start = ((), (), s32[]{:S(2)}) async-start(), calls=%async_computation.2 | async-start | bytes 655360 | tf_op jit(solution)/shard_map/reduce_scatter | solution.py:83
  734.8 62.5 %reduce-scatter.5.cloned.1.call-start = ((), (), s32[]{:S(2)}) async-start(), calls=%async_computation.3 | async-start | bytes 655360 | tf_op jit(solution)/shard_map/reduce_scatter | solution.py:86
  743.4 4.0 copy-start.2
Sparse Core Ops, SparseCore 0:
  366.6 364.4 all-reduce.4
  734.9 40.1 reduce-scatter.2
  778.1 19.1 reduce-scatter.4
where the time goes:
time: 806 us; the launch traced here: 804 us
  waiting for transfers between devices  406 us (50%)
  blocking collectives  206 us (26%)
  matrix products  157 us (19%)
  between operations  13.8 us (2%)
  local copies, waits for them, and re-layouts  12.6 us (2%)
    psum x1, waiting for transfers between devices, body(): lax.psum(dkp_part.astype(jnp.bfloat16), 'seq').astype(jnp.float32)  365 us
    psum x1, blocking collectives, body(): kp_full, vp_full = lax.psum((kp_part, vp_part), 'seq')  206 us
    dot_general x16, matrix products, per_head(): jnp.dot(grad_scores, kp_head, preferred_element_type=jnp.float32)  30.7 us
    dot_general x16, matrix products, per_head(): lax.dot_general(probs_low, g_head, (((0,), (0,)), ((), ())), preferred_el...  30.3 us
    dot_general x16, matrix products, per_head(): lax.dot_general(grad_scores, q_head, (((0,), (0,)), ((), ())), preferred_...  29.9 us
    reduce_scatter x1, waiting for transfers between devices, body(): lax.psum_scatter(term_value.astype(jnp.bfloat16), 'dp', scatter_dimension...  22.1 us
    dot_general x16, matrix products, per_head(): lax.dot_general(g_head, vp_head, (((1,), (1,)), ((), ())), preferred_elem...  20.7 us
    dot_general x16, matrix products, per_head(): lax.dot_general(q_head, kp_head, (((1,), (1,)), ((), ())), preferred_elem...  20.5 us
  transfers between devices with their start and end apart: 3, of which 3 were waited for; matrix products, arithmetic and copies ran while one was open for 3% of the time, Pallas kernels for 0%

commit v1 on v0

v1 whole, which is shorter than its diff:
```python
import functools

import jax
import jax.numpy as jnp
from jax import lax
from jax.experimental import pallas as pl
from jax.experimental.pallas import tpu as pltpu
from jax.sharding import PartitionSpec as P

H = 16
HEAD_DIM = 128
SCALE = HEAD_DIM ** (-0.5)
N_SEQ = 32
N_DP = 4
F32 = jnp.float32
BF16 = jnp.bfloat16


def dot(a, b, dims):
    return lax.dot_general(a, b, (dims, ((), ())), preferred_element_type=F32)


def probs_kernel(q_ref, g_ref, kp_ref, dvp_ref, top_ref, inv_ref):
    scores = dot(kp_ref[...], q_ref[...], ((1,), (1,))) * SCALE
    top = jnp.max(scores, axis=0, keepdims=True)
    e = jnp.exp(scores - top)
    inv = 1.0 / jnp.sum(e, axis=0, keepdims=True)
    probs_low = (e * inv).astype(BF16)
    dvp_ref[...] = dot(probs_low, g_ref[...], ((1,), (0,))).astype(BF16)
    top_ref[0] = top
    inv_ref[0] = inv


def scores_kernel(q_ref, g_ref, kp_ref, vp_ref, top_ref, inv_ref, gq_ref, dkp_ref):
    scores = dot(kp_ref[...], q_ref[...], ((1,), (1,))) * SCALE
    probs = jnp.exp(scores - top_ref[0]) * inv_ref[0]
    grad_probs = dot(vp_ref[...], g_ref[...], ((1,), (1,)))
    delta = jnp.sum(probs * grad_probs, axis=0, keepdims=True)
    grad_scores = (probs * (grad_probs - delta) * SCALE).astype(BF16)
    dkp_ref[...] = dot(grad_scores, q_ref[...], ((1,), (0,))).astype(BF16)
    gq_t = dot(kp_ref[...], grad_scores, ((0,), (0,)))
    gq_ref[...] = gq_t.T.astype(BF16)


def head_block(rows):
    return pl.BlockSpec((rows, HEAD_DIM), lambda h: (0, h))


def stat_block(rows):
    return pl.BlockSpec((1, 1, rows), lambda h: (h, 0, 0))


def probs_call(q, g, kp):
    rows, feats = q.shape
    n = kp.shape[0]
    stat = jax.ShapeDtypeStruct((H, 1, rows), F32)
    return pl.pallas_call(
        probs_kernel,
        grid=(H,),
        in_specs=[head_block(rows), head_block(rows), head_block(n)],
        out_specs=[head_block(n), stat_block(rows), stat_block(rows)],
        out_shape=[jax.ShapeDtypeStruct((n, feats), BF16), stat, stat],
        compiler_params=pltpu.CompilerParams(vmem_limit_bytes=40 * 2**20),
        cost_estimate=pl.CostEstimate(
            flops=4 * rows * n * feats, bytes_accessed=8 * rows * feats, transcendentals=H * rows * n
        ),
    )(q, g, kp)


def scores_call(q, g, kp, vp, top, inv):
    rows, feats = q.shape
    n = kp.shape[0]
    return pl.pallas_call(
        scores_kernel,
        grid=(H,),
        in_specs=[
            head_block(rows),
            head_block(rows),
            head_block(n),
            head_block(n),
            stat_block(rows),
            stat_block(rows),
        ],
        out_specs=[head_block(rows), head_block(n)],
        out_shape=[
            jax.ShapeDtypeStruct((rows, feats), BF16),
            jax.ShapeDtypeStruct((n, feats), BF16),
        ],
        compiler_params=pltpu.CompilerParams(vmem_limit_bytes=40 * 2**20),
        cost_estimate=pl.CostEstimate(
            flops=8 * rows * n * feats, bytes_accessed=12 * rows * feats, transcendentals=H * rows * n
        ),
    )(q, g, kp, vp, top, inv)


def back_kernel(p_ref, d_ref, o_ref):
    o_ref[...] = dot(p_ref[...], d_ref[...], ((0,), (0,))).astype(BF16)


def back_call(proj, d):
    n, rows = proj.shape
    feats = d.shape[1]
    wide = 512
    return pl.pallas_call(
        back_kernel,
        grid=(feats // wide,),
        in_specs=[
            pl.BlockSpec((n, rows), lambda i: (0, 0)),
            pl.BlockSpec((n, wide), lambda i: (0, i)),
        ],
        out_specs=pl.BlockSpec((rows, wide), lambda i: (0, i)),
        out_shape=jax.ShapeDtypeStruct((rows, feats), BF16),
        compiler_params=pltpu.CompilerParams(vmem_limit_bytes=40 * 2**20),
        cost_estimate=pl.CostEstimate(
            flops=2 * rows * n * feats, bytes_accessed=4 * rows * feats, transcendentals=0
        ),
    )(proj, d)


def all_sum(part):
    n, feats = part.shape
    own = n // N_SEQ
    got = lax.all_to_all(part.reshape(N_SEQ, own, feats), "seq", 0, 0)
    total = jnp.sum(got.astype(F32), axis=0).astype(BF16)
    full = lax.all_to_all(jnp.broadcast_to(total[None], (N_SEQ, own, feats)), "seq", 0, 0)
    return full.reshape(n, feats)


def dp_sum(term):
    n, rows = term.shape
    got = lax.all_to_all(term.reshape(N_DP, n // N_DP, rows), "dp", 0, 0)
    return jnp.sum(got.astype(F32), axis=0).astype(BF16)


def body(query, key, value, grad_ctx, proj_key, proj_value):
    q, k, v, g = query[0], key[0], value[0], grad_ctx[0]
    kp = all_sum(dot(proj_key, k, ((1,), (0,))).astype(BF16))
    vp = all_sum(dot(proj_value, v, ((1,), (0,))).astype(BF16))
    dvp_part, top, inv = probs_call(q, g, kp)
    dvp = all_sum(dvp_part)
    gq, dkp_part = scores_call(q, g, kp, vp, top, inv)
    dkp = all_sum(dkp_part)
    sum_v = dp_sum(dot(dvp, v, ((1,), (1,))).astype(BF16))
    sum_k = dp_sum(dot(dkp, k, ((1,), (1,))).astype(BF16))
    grad_v = back_call(proj_value, dvp)
    grad_k = back_call(proj_key, dkp)
    return gq[None], grad_k[None], grad_v[None], sum_k, sum_v


def solution(mesh):
    block = P("dp", "seq", None)
    return jax.shard_map(
        body,
        mesh=mesh,
        in_specs=(block, block, block, block, P(None, "seq"), P(None, "seq")),
        out_specs=(block, block, block, P("dp", "seq"), P("dp", "seq")),
        check_vma=False,
    )
```

time: 806 us -> 328 us (0.41)
  waiting for transfers between devices: 406 us -> 170 us
  blocking collectives: 206 us -> 0 us
  matrix products: 157 us -> 15 us
  starting transfers between devices: 0.12 us -> 70.8 us
  Pallas kernels: 0 us -> 43.4 us
  between operations: 13.8 us -> 0.77 us
    psum x1 -> x0, waiting for transfers between devices: 365 us -> none  [body(): lax.psum(dkp_part.astype(jnp.bfloat16), 'seq').astype(jnp.float32)]
    psum x1 -> x0, blocking collectives: 206 us -> none  [body(): kp_full, vp_full = lax.psum((kp_part, vp_part), 'seq')]
    all_to_all x0 -> x10, waiting for transfers between devices: none -> 170 us  [the longest x4 84.6 us: all_sum(): lax.all_to_all(jnp.broadcast_to(total[None], (N_SEQ, own, feats)), 'seq',...]
    dot_general x86 -> x4, matrix products: 157 us -> 15 us  [dot(): return lax.dot_general(a, b, (dims, ((), ())), preferred_element_type=F32)]
    all_to_all x0 -> x10, starting transfers between devices: none -> 70.8 us  [the longest x4 32.3 us: all_sum(): got = lax.all_to_all(part.reshape(N_SEQ, own, feats), 'seq', 0, 0)]
    pallas_call x0 -> x4, Pallas kernels: none -> 43.4 us  [the longest x1 18.5 us: scores_call(): pl.pallas_call(scores_kernel, grid=(H,), in_specs=[head_block(rows), head...]
    reduce_scatter x2 -> x0, waiting for transfers between devices: 41.8 us -> none  [the longest x1 22.1 us: body(): lax.psum_scatter(term_value.astype(jnp.bfloat16), 'dp', scatter_dimension...]
  transfers between devices with their start and end apart: 3 -> 10, of which waited for: 3 -> 9; matrix products, arithmetic and copies ran while one was open for 3% -> 6% of each run, Pallas kernels for 0% -> 13%
where the time goes in v1:
time: 328 us; the launch traced here: 326 us
  waiting for transfers between devices  170 us (52%)
  starting transfers between devices  70.8 us (22%)
  Pallas kernels  43.4 us (13%)
  local copies, waits for them, and re-layouts  15.3 us (5%)
  matrix products  15 us (5%)
  other arithmetic  10.2 us (3%)
    all_to_all x4, waiting for transfers between devices, all_sum(): lax.all_to_all(jnp.broadcast_to(total[None], (N_SEQ, own, feats)), 'seq',...  84.6 us
    all_to_all x4, waiting for transfers between devices, all_sum(): got = lax.all_to_all(part.reshape(N_SEQ, own, feats), 'seq', 0, 0)  82.1 us
    all_to_all x4, starting transfers between devices, all_sum(): got = lax.all_to_all(part.reshape(N_SEQ, own, feats), 'seq', 0, 0)  32.3 us
    all_to_all x4, starting transfers between devices, all_sum(): lax.all_to_all(jnp.broadcast_to(total[None], (N_SEQ, own, feats)), 'seq',...  28.3 us
    pallas_call x1, Pallas kernels, scores_call(): pl.pallas_call(scores_kernel, grid=(H,), in_specs=[head_block(rows), head...  18.5 us
    pallas_call x1, Pallas kernels, probs_call(): pl.pallas_call(probs_kernel, grid=(H,), in_specs=[head_block(rows), head_...  15.6 us
    dot_general x4, matrix products, dot(): return lax.dot_general(a, b, (dims, ((), ())), preferred_element_type=F32)  15 us
    all_to_all x2, starting transfers between devices, dp_sum(): got = lax.all_to_all(term.reshape(N_DP, n // N_DP, rows), 'dp', 0, 0)  10.1 us
  transfers between devices with their start and end apart: 10, of which 9 were waited for; matrix products, arithmetic and copies ran while one was open for 6% of the time, Pallas kernels for 13%

profile of v1, /device:TPU:1, one launch (start us, length us, event | category | flops | bytes accessed | tf_op | source)
XLA Modules:
  0.0 325.8 jit_solution(11068057162188744311)
XLA Ops:
  0.6 0.0 copy-start
  0.6 4.5 %convolution_convert_fusion.1 = bf16[512,2048]{1,0:T(8,128)(2,1)} fusion(bf16[512,512]{1,0:T(8,128)(2,1)} %p_ref.2, bf16[1,512,2048]{2,1,0:T(8,128)(2,1)} %param.7), kind=kOutput, calls=%fused_computation.1 | convolution fusion | flops 1074790400 | bytes 4718592 | tf_op jit(solution)/shard_map/dot_general | solution.py:20
  5.1 11.6 %all-to-all-start = ((bf16[32,16,2048]{2,1,0:T(8,128)(2,1)}), bf16[32,16,2048]{2,1,0:T(8,128)(2,1)}, u32[]{:S(2)}, u32[]{:S(2)}) async-start(bf16[32,16,2048]{2,1,0:T(8,128)(2,1)} %bitcast.42), calls=%async_computation | async-start | bytes 4194304 | tf_op jit(solution)/shard_map/all_to_all | solution.py:123
  16.8 2.6 convolution_convert_fusion
  19.3 25.3 %all-to-all-done = bf16[32,16,2048]{2,1,0:T(8,128)(2,1)} async-done(((bf16[32,16,2048]{2,1,0:T(8,128)(2,1)}), bf16[32,16,2048]{2,1,0:T(8,128)(2,1)}, u32[]{:S(2)}, u32[]{:S(2)}) %all-to-all-start) | async-done | bytes 2097184 | tf_op jit(solution)/shard_map/all_to_all | solution.py:123
  44.6 7.0 %all-to-all-start.2 = ((bf16[32,16,2048]{2,1,0:T(8,128)(2,1)}), bf16[32,16,2048]{2,1,0:T(8,128)(2,1)}, u32[]{:S(2)}, u32[]{:S(2)}) async-start(bf16[32,16,2048]{2,1,0:T(8,128)(2,1)} %bitcast.41), calls=%async_computation.2 | async-start | bytes 4194304 | tf_op jit(solution)/shard_map/all_to_all | solution.py:123
  51.6 1.9 reduce_sum.72
  53.5 26.0 %all-to-all-done.2 = bf16[32,16,2048]{2,1,0:T(8,128)(2,1)} async-done(((bf16[32,16,2048]{2,1,0:T(8,128)(2,1)}), bf16[32,16,2048]{2,1,0:T(8,128)(2,1)}, u32[]{:S(2)}, u32[]{:S(2)}) %all-to-all-start.2) | async-done | bytes 2097184 | tf_op jit(solution)/shard_map/all_to_all | solution.py:123
  79.5 1.6 broadcast_in_dim.14
  81.1 7.0 %all-to-all-start.1 = ((bf16[32,16,2048]{2,1,0:T(8,128)(2,1)}), bf16[32,16,2048]{2,1,0:T(8,128)(2,1)}, u32[]{:S(2)}, u32[]{:S(2)}) async-start(bf16[32,16,2048]{2,1,0:T(8,128)(2,1)} %broadcast_in_dim.14), calls=%async_computation.1 | async-start | bytes 4194304 | tf_op jit(solution)/shard_map/all_to_all | solution.py:125
  88.0 1.9 reduce_sum.73
  89.9 25.9 %all-to-all-done.1 = bf16[32,16,2048]{2,1,0:T(8,128)(2,1)} async-done(((bf16[32,16,2048]{2,1,0:T(8,128)(2,1)}), bf16[32,16,2048]{2,1,0:T(8,128)(2,1)}, u32[]{:S(2)}, u32[]{:S(2)}) %all-to-all-start.1) | async-done | bytes 2097184 | tf_op jit(solution)/shard_map/all_to_all | solution.py:125
  115.9 1.6 broadcast_in_dim.15
  117.4 7.2 %all-to-all-start.3 = ((bf16[32,16,2048]{2,1,0:T(8,128)(2,1)}), bf16[32,16,2048]{2,1,0:T(8,128)(2,1)}, u32[]{:S(2)}, u32[]{:S(2)}) async-start(bf16[32,16,2048]{2,1,0:T(8,128)(2,1)} %broadcast_in_dim.15), calls=%async_computation.3 | async-start | bytes 4194304 | tf_op jit(solution)/shard_map/all_to_all | solution.py:125
  124.6 0.0 copy-start.5
  124.6 1.6 copy-done.5
  126.2 1.6 copy-done.7
  127.8 15.6 %shard_map.101 = (bf16[512,2048]{1,0:T(8,128)(2,1)S(1)}, f32[16,1,512]{2,1,0:T(1,128)S(1)}, f32[16,1,512]{2,1,0:T(1,128)S(1)}) custom-call(bf16[512,2048]{1,0:T(8,128)(2,1)S(1)} %bitcast.35, bf16[512,2048]{1,0:T(8,128)(2,1)S(1)} %bitcast.37, bf16[512,2048]{1,0:T(8,128)(2,1)} %bitcast.4.kp_ref), custom_call_target="tpu_custom_call" | custom-call | flops 2147483648 | bytes 8388608 | tf_op jit(solution)/shard_map/pallas_call | solution.py:57
  143.4 0.0 copy-start.1
  143.4 1.3 copy-done.1
  144.7 8.2 %all-to-all-done.3 = bf16[32,16,2048]{2,1,0:T(8,128)(2,1)} async-done(((bf16[32,16,2048]{2,1,0:T(8,128)(2,1)}), bf16[32,16,2048]{2,1,0:T(8,128)(2,1)}, u32[]{:S(2)}, u32[]{:S(2)}) %all-to-all-start.3) | async-done | bytes 2097184 | tf_op jit(solution)/shard_map/all_to_all | solution.py:125
  152.9 6.6 %all-to-all-start.6 = ((bf16[32,16,2048]{2,1,0:T(8,128)(2,1)}), bf16[32,16,2048]{2,1,0:T(8,128)(2,1)}, u32[]{:S(2)}, u32[]{:S(2)}) async-start(bf16[32,16,2048]{2,1,0:T(8,128)(2,1)} %bitcast.33), calls=%async_computation.6 | async-start | bytes 4194304 | tf_op jit(solution)/shard_map/all_to_all | solution.py:123
  159.5 0.0 copy-start.6
  159.5 1.6 copy-done.6
  161.1 1.6 copy-done.8
  162.7 18.5 %shard_map.102 = (bf16[512,2048]{1,0:T(8,128)(2,1)}, bf16[512,2048]{1,0:T(8,128)(2,1)S(1)}) custom-call(bf16[512,2048]{1,0:T(8,128)(2,1)S(1)} %bitcast.36, bf16[512,2048]{1,0:T(8,128)(2,1)S(1)} %bitcast.38, bf16[512,2048]{1,0:T(8,128)(2,1)} %bitcast.4.kp_ref, bf16[512,2048]{1,0:T(8,128)(2,1)} %bitcast.7.vp_ref, f32[16,1,512]{2,1,0:T(1,128)S(1)} %get-tuple-element.10.top_ref, ...), custom_call_target="tpu_custom_call" | custom-call | flops 4294967296 | bytes 12582912 | tf_op jit(solution)/shard_map/pallas_call | solution.py:73
  181.1 1.3 copy-done.2
  182.5 4.9 %all-to-all-done.6 = bf16[32,16,2048]{2,1,0:T(8,128)(2,1)} async-done(((bf16[32,16,2048]{2,1,0:T(8,128)(2,1)}), bf16[32,16,2048]{2,1,0:T(8,128)(2,1)}, u32[]{:S(2)}, u32[]{:S(2)}) %all-to-all-start.6) | async-done | bytes 2097184 | tf_op jit(solution)/shard_map/all_to_all | solution.py:123
  187.3 7.2 %all-to-all-start.4 = ((bf16[32,16,2048]{2,1,0:T(8,128)(2,1)}), bf16[32,16,2048]{2,1,0:T(8,128)(2,1)}, u32[]{:S(2)}, u32[]{:S(2)}) async-start(bf16[32,16,2048]{2,1,0:T(8,128)(2,1)} %bitcast.34), calls=%async_computation.4 | async-start | bytes 4194304 | tf_op jit(solution)/shard_map/all_to_all | solution.py:123
  194.5 1.9 reduce_sum.75
  196.4 26.0 %all-to-all-done.4 = bf16[32,16,2048]{2,1,0:T(8,128)(2,1)} async-done(((bf16[32,16,2048]{2,1,0:T(8,128)(2,1)}), bf16[32,16,2048]{2,1,0:T(8,128)(2,1)}, u32[]{:S(2)}, u32[]{:S(2)}) %all-to-all-start.4) | async-done | bytes 2097184 | tf_op jit(solution)/shard_map/all_to_all | solution.py:123
  222.4 1.6 broadcast_in_dim.38
  224.0 6.9 %all-to-all-start.7 = ((bf16[32,16,2048]{2,1,0:T(8,128)(2,1)}), bf16[32,16,2048]{2,1,0:T(8,128)(2,1)}, u32[]{:S(2)}, u32[]{:S(2)}) async-start(bf16[32,16,2048]{2,1,0:T(8,128)(2,1)} %broadcast_in_dim.38), calls=%async_computation.7 | async-start | bytes 4194304 | tf_op jit(solution)/shard_map/all_to_all | solution.py:125
  231.0 1.9 reduce_sum.74
  232.9 25.9 %all-to-all-done.7 = bf16[32,16,2048]{2,1,0:T(8,128)(2,1)} async-done(((bf16[32,16,2048]{2,1,0:T(8,128)(2,1)}), bf16[32,16,2048]{2,1,0:T(8,128)(2,1)}, u32[]{:S(2)}, u32[]{:S(2)}) %all-to-all-start.7) | async-done | bytes 2097184 | tf_op jit(solution)/shard_map/all_to_all | solution.py:125
  258.8 1.6 broadcast_in_dim.17
  260.3 7.2 %all-to-all-start.5 = ((bf16[32,16,2048]{2,1,0:T(8,128)(2,1)}), bf16[32,16,2048]{2,1,0:T(8,128)(2,1)}, u32[]{:S(2)}, u32[]{:S(2)}) async-start(bf16[32,16,2048]{2,1,0:T(8,128)(2,1)} %broadcast_in_dim.17), calls=%async_computation.5 | async-start | bytes 4194304 | tf_op jit(solution)/shard_map/all_to_all | solution.py:125
  267.6 3.7 %fusion.9 = bf16[512,512]{1,0:T(8,128)(2,1)} fusion(bf16[512,2048]{1,0:T(8,128)(2,1)} %bitcast.13.d_ref, bf16[1,512,2048]{2,1,0:T(8,128)(2,1)S(1)} %copy-done), kind=kOutput, calls=%fused_computation.9 | convolution fusion | flops 1074003968 | bytes 4718592 | tf_op jit(solution)/shard_map/dot_general | solution.py:20
  271.2 24.6 %all-to-all-done.5 = bf16[32,16,2048]{2,1,0:T(8,128)(2,1)} async-done(((bf16[32,16,2048]{2,1,0:T(8,128)(2,1)}), bf16[32,16,2048]{2,1,0:T(8,128)(2,1)}, u32[]{:S(2)}, u32[]{:S(2)}) %all-to-all-start.5) | async-done | bytes 2097184 | tf_op jit(solution)/shard_map/all_to_all | solution.py:125
  295.8 5.1 %all-to-all-start.9 = ((bf16[4,128,512]{2,1,0:T(8,128)(2,1)}), bf16[4,128,512]{2,1,0:T(8,128)(2,1)S(1)}, u32[]{:S(2)}, u32[]{:S(2)}) async-start(bf16[4,128,512]{2,1,0:T(8,128)(2,1)} %bitcast.44), calls=%async_computation.9 | async-start | bytes 1048576 | tf_op jit(solution)/shard_map/all_to_all | solution.py:131
  301.0 4.3 %fusion.6 = bf16[512,512]{1,0:T(8,128)(2,1)} fusion(bf16[512,2048]{1,0:T(8,128)(2,1)} %bitcast.10.d_ref, bf16[1,512,2048]{2,1,0:T(8,128)(2,1)} %param.7), kind=kOutput, calls=%fused_computation.8 | convolution fusion | flops 1074003968 | bytes 4718592 | tf_op jit(solution)/shard_map/dot_general | solution.py:20
  305.3 3.7 %all-to-all-done.9 = bf16[4,128,512]{2,1,0:T(8,128)(2,1)S(1)} async-done(((bf16[4,128,512]{2,1,0:T(8,128)(2,1)}), bf16[4,128,512]{2,1,0:T(8,128)(2,1)S(1)}, u32[]{:S(2)}, u32[]{:S(2)}) %all-to-all-start.9) | async-done | bytes 524320 | tf_op jit(solution)/shard_map/all_to_all | solution.py:131
  309.0 5.0 %all-to-all-start.8 = ((bf16[4,128,512]{2,1,0:T(8,128)(2,1)}), bf16[4,128,512]{2,1,0:T(8,128)(2,1)}, u32[]{:S(2)}, u32[]{:S(2)}) async-start(bf16[4,128,512]{2,1,0:T(8,128)(2,1)} %bitcast.43), calls=%async_computation.8 | async-start | bytes 1048576 | tf_op jit(solution)/shard_map/all_to_all | solution.py:131
  313.9 4.7 %shard_map.104 = bf16[512,2048]{1,0:T(8,128)(2,1)} custom-call(bf16[512,512]{1,0:T(8,128)(2,1)S(1)} %copy-done.3, bf16[512,2048]{1,0:T(8,128)(2,1)} %bitcast.13.d_ref), custom_call_target="tpu_custom_call" | custom-call | flops 1073741824 | bytes 4194304 | tf_op jit(solution)/shard_map/pallas_call | solution.py:104
  318.6 4.6 %shard_map.103 = bf16[512,2048]{1,0:T(8,128)(2,1)} custom-call(bf16[512,512]{1,0:T(8,128)(2,1)S(1)} %copy-done.4, bf16[512,2048]{1,0:T(8,128)(2,1)} %bitcast.10.d_ref), custom_call_target="tpu_custom_call" | custom-call | flops 1073741824 | bytes 4194304 | tf_op jit(solution)/shard_map/pallas_call | solution.py:104
  323.3 0.7 reduce_sum.77
  324.0 0.0 all-to-all-done.8
  324.0 1.8 reduce_sum.76
  (8 shorter events, 0.0 us)
Async XLA Ops:
  0.6 16.1 %copy-start = (bf16[1,512,2048]{2,1,0:T(8,128)(2,1)S(1)}, bf16[1,512,2048]{2,1,0:T(8,128)(2,1)}, u32[]{:S(2)}) copy-start(bf16[1,512,2048]{2,1,0:T(8,128)(2,1)} %param.8) | copy-start | bytes 6291460
  5.1 11.6 %copy-start.3 = (bf16[512,512]{1,0:T(8,128)(2,1)S(1)}, bf16[512,512]{1,0:T(8,128)(2,1)}, u32[]{:S(2)}) copy-start(bf16[512,512]{1,0:T(8,128)(2,1)} %p_ref.3) | copy-start | bytes 1572868
  5.1 39.5 %all-to-all-start = ((bf16[32,16,2048]{2,1,0:T(8,128)(2,1)}), bf16[32,16,2048]{2,1,0:T(8,128)(2,1)}, u32[]{:S(2)}, u32[]{:S(2)}) async-start(bf16[32,16,2048]{2,1,0:T(8,128)(2,1)} %bitcast.42), calls=%async_computation | async-start | bytes 4194304 | tf_op jit(solution)/shard_map/all_to_all | solution.py:123
  44.6 34.9 %all-to-all-start.2 = ((bf16[32,16,2048]{2,1,0:T(8,128)(2,1)}), bf16[32,16,2048]{2,1,0:T(8,128)(2,1)}, u32[]{:S(2)}, u32[]{:S(2)}) async-start(bf16[32,16,2048]{2,1,0:T(8,128)(2,1)} %bitcast.41), calls=%async_computation.2 | async-start | bytes 4194304 | tf_op jit(solution)/shard_map/all_to_all | solution.py:123
  81.1 34.8 %all-to-all-start.1 = ((bf16[32,16,2048]{2,1,0:T(8,128)(2,1)}), bf16[32,16,2048]{2,1,0:T(8,128)(2,1)}, u32[]{:S(2)}, u32[]{:S(2)}) async-start(bf16[32,16,2048]{2,1,0:T(8,128)(2,1)} %broadcast_in_dim.14), calls=%async_computation.1 | async-start | bytes 4194304 | tf_op jit(solution)/shard_map/all_to_all | solution.py:125
  117.4 35.5 %all-to-all-start.3 = ((bf16[32,16,2048]{2,1,0:T(8,128)(2,1)}), bf16[32,16,2048]{2,1,0:T(8,128)(2,1)}, u32[]{:S(2)}, u32[]{:S(2)}) async-start(bf16[32,16,2048]{2,1,0:T(8,128)(2,1)} %broadcast_in_dim.15), calls=%async_computation.3 | async-start | bytes 4194304 | tf_op jit(solution)/shard_map/all_to_all | solution.py:125
  124.6 1.6 copy-start.5
  126.2 1.6 copy-start.7
  143.4 1.3 copy-start.1
  152.9 34.4 %all-to-all-start.6 = ((bf16[32,16,2048]{2,1,0:T(8,128)(2,1)}), bf16[32,16,2048]{2,1,0:T(8,128)(2,1)}, u32[]{:S(2)}, u32[]{:S(2)}) async-start(bf16[32,16,2048]{2,1,0:T(8,128)(2,1)} %bitcast.33), calls=%async_computation.6 | async-start | bytes 4194304 | tf_op jit(solution)/shard_map/all_to_all | solution.py:123
  159.5 1.6 copy-start.6
  161.1 1.6 copy-start.8
  181.1 1.3 copy-start.2
  187.3 35.1 %all-to-all-start.4 = ((bf16[32,16,2048]{2,1,0:T(8,128)(2,1)}), bf16[32,16,2048]{2,1,0:T(8,128)(2,1)}, u32[]{:S(2)}, u32[]{:S(2)}) async-start(bf16[32,16,2048]{2,1,0:T(8,128)(2,1)} %bitcast.34), calls=%async_computation.4 | async-start | bytes 4194304 | tf_op jit(solution)/shard_map/all_to_all | solution.py:123
  224.0 34.7 %all-to-all-start.7 = ((bf16[32,16,2048]{2,1,0:T(8,128)(2,1)}), bf16[32,16,2048]{2,1,0:T(8,128)(2,1)}, u32[]{:S(2)}, u32[]{:S(2)}) async-start(bf16[32,16,2048]{2,1,0:T(8,128)(2,1)} %broadcast_in_dim.38), calls=%async_computation.7 | async-start | bytes 4194304 | tf_op jit(solution)/shard_map/all_to_all | solution.py:125
  260.3 35.5 %all-to-all-start.5 = ((bf16[32,16,2048]{2,1,0:T(8,128)(2,1)}), bf16[32,16,2048]{2,1,0:T(8,128)(2,1)}, u32[]{:S(2)}, u32[]{:S(2)}) async-start(bf16[32,16,2048]{2,1,0:T(8,128)(2,1)} %broadcast_in_dim.17), calls=%async_computation.5 | async-start | bytes 4194304 | tf_op jit(solution)/shard_map/all_to_all | solution.py:125
  295.8 13.1 %all-to-all-start.9 = ((bf16[4,128,512]{2,1,0:T(8,128)(2,1)}), bf16[4,128,512]{2,1,0:T(8,128)(2,1)S(1)}, u32[]{:S(2)}, u32[]{:S(2)}) async-start(bf16[4,128,512]{2,1,0:T(8,128)(2,1)} %bitcast.44), calls=%async_computation.9 | async-start | bytes 1048576 | tf_op jit(solution)/shard_map/all_to_all | solution.py:131
  309.0 15.0 %all-to-all-start.8 = ((bf16[4,128,512]{2,1,0:T(8,128)(2,1)}), bf16[4,128,512]{2,1,0:T(8,128)(2,1)}, u32[]{:S(2)}, u32[]{:S(2)}) async-start(bf16[4,128,512]{2,1,0:T(8,128)(2,1)} %bitcast.43), calls=%async_computation.8 | async-start | bytes 1048576 | tf_op jit(solution)/shard_map/all_to_all | solution.py:131
  313.9 4.7 %copy-start.4 = (bf16[512,512]{1,0:T(8,128)(2,1)S(1)}, bf16[512,512]{1,0:T(8,128)(2,1)}, u32[]{:S(2)}) copy-start(bf16[512,512]{1,0:T(8,128)(2,1)} %p_ref.2) | copy-start | bytes 1572868
